TPU v7x, 256 devices: a whole 4x4x8 slice. The times are simulated.
256 devices in a mesh: prow: 16 (over x, y), pcol: 16 (over z, core).
Axes of the slice: x: 4, y: 4, z: 8, core: 2. Of those that a mesh axis runs over, the one named last changes fastest.
Arguments:
- known_inverse: bfloat16 [32768, 16, 16, 128], P('prow', None, 'pcol'), may hold values from -6 to 6
- pattern: int32 [256, 16, 16, 1], P('prow', None, 'pcol'), may hold values 0 or 1
- panel_one: bfloat16 [32768, 512], P(('prow', 'pcol')), may hold values from -0.03125 to 0.03125
- panel_two: bfloat16 [32768, 512], P(('prow', 'pcol')), may hold values from -0.03125 to 0.03125
- panel_top: bfloat16 [512, 512], replicated, may hold values from -0.25 to 0.25
- structure: int32 [32768], P(('prow', 'pcol')), may hold values from 0 to 1, as said below
- diag_one: bfloat16 [512, 512], replicated, may hold values from -6 to 6
- diag_two: bfloat16 [512, 512], replicated, may hold values from -6 to 6
Outputs:
- inverse_one: bfloat16 [32768, 512], P(('prow', 'pcol'))
- corner_one: bfloat16 [512, 512], replicated
- inverse_top: bfloat16 [512, 512], replicated
- inverse_two: bfloat16 [32768, 512], P(('prow', 'pcol'))
- corner_two: bfloat16 [512, 512], replicated
Inputs may be any that keep to these rules, and one draw needn't show every extreme that they name: `structure`: in every aligned pair of rows (2 k and 2 k + 1) at least one entry is 1.
All inputs are finite; a program needn't handle non-finite values. No bound on the sum of `pattern` on one device may be relied on, other than what follows from the above.
Results may differ from a plain program's by a relative error of at most 0.0058.
Values may be sent and summed in bfloat16 or wider, within the bound.
A program may use at most 128 MiB of HBM per device.

v0:
```python
import jax
import jax.numpy as jnp
from jax import lax
from jax.sharding import PartitionSpec as P

BLK = 128


def on_device(
    known_inverse, pattern, panel_one, panel_two, panel_top, structure, diag_one, diag_two
):
    row_count = known_inverse.shape[0]
    col_groups = known_inverse.shape[1]
    piece_rows = known_inverse.shape[3]
    block_rows = row_count // BLK
    piece_blocks = piece_rows // BLK
    shaped = known_inverse.reshape(block_rows, BLK, col_groups, piece_blocks, BLK)
    flag_table = pattern.reshape(block_rows, 1, col_groups, piece_blocks, 1)
    masked = jnp.where(flag_table > 0, shaped, jnp.zeros_like(shaped)).reshape(
        row_count, col_groups * piece_rows
    )
    row_flags = structure.reshape(piece_rows, 1) > 0
    masked_two = jnp.where(row_flags, panel_two, jnp.zeros_like(panel_two))

    def accumulate(pieces):
        return jnp.dot(masked, pieces, preferred_element_type=jnp.float32)

    partial_one = accumulate(lax.all_gather(panel_one, "prow", axis=0, tiled=True))
    reduced_one = lax.psum_scatter(partial_one, "pcol", scatter_dimension=0, tiled=True)
    partial_two = accumulate(lax.all_gather(masked_two, "prow", axis=0, tiled=True))
    reduced_two = lax.psum_scatter(partial_two, "pcol", scatter_dimension=0, tiled=True)
    inverse_one = (-reduced_one).astype(jnp.bfloat16)
    own_term = jnp.dot(panel_one.T, inverse_one, preferred_element_type=jnp.float32)
    cross_local = jnp.dot(inverse_one.T, masked_two, preferred_element_type=jnp.float32)
    lower_two = -(reduced_two + jnp.dot(inverse_one, panel_top, preferred_element_type=jnp.float32))
    inverse_two = jnp.where(row_flags, lower_two, jnp.zeros_like(lower_two)).astype(jnp.bfloat16)
    tail_local = jnp.dot(masked_two.T, inverse_two, preferred_element_type=jnp.float32)
    top_weights = panel_top.astype(jnp.float32)
    own_sum, cross_sum = lax.psum((own_term, cross_local), ("prow", "pcol"))
    corner_full = diag_one.astype(jnp.float32) - own_sum
    top_value = jnp.dot(corner_full, top_weights, precision=lax.Precision.HIGHEST) + cross_sum
    inverse_top = (-top_value).astype(jnp.bfloat16)
    tail_sum = lax.psum(tail_local, ("prow", "pcol"))
    corner_two = (
        diag_two.astype(jnp.float32)
        - jnp.dot(panel_top.T, inverse_top, preferred_element_type=jnp.float32)
        - tail_sum
    )
    return (
        inverse_one,
        corner_full.astype(jnp.bfloat16),
        inverse_top,
        inverse_two,
        corner_two.astype(jnp.bfloat16),
    )


def solution(mesh):
    in_specs = (
        P("prow", None, "pcol", None),
        P("prow", None, "pcol", None),
        P(("prow", "pcol"), None),
        P(("prow", "pcol"), None),
        P(),
        P(("prow", "pcol")),
        P(),
        P(),
    )
    out_specs = (P(("prow", "pcol"), None), P(), P(), P(("prow", "pcol"), None), P())
    return jax.shard_map(
        on_device, mesh=mesh, in_specs=in_specs, out_specs=out_specs, check_vma=False
    )
```

profile of v0, /device:TPU:8, one launch (start us, length us, event | category | flops | bytes accessed | tf_op | source)
XLA Modules:
  0.0 526.8 jit_solution(959092906501539637)
XLA Ops:
  7.2 0.7 all-gather.3.cloned.1.call-update
  8.0 0.7 broadcast_compare_fusion.1
  8.6 1.6 broadcast_select_fusion
  10.3 0.7 broadcast_compare_fusion
  11.1 51.9 %all-gather.3.cloned.1.call-done = bf16[2048,512]{1,0:T(8,128)(2,1)} async-done(((bf16[128,512]{1,0:T(8,128)(2,1)}), bf16[2048,512]{1,0:T(8,128)(2,1)}) %all-gather.3.cloned.1.call-update) | async-done | bytes 2097168 | tf_op jit(solution)/shard_map/all_gather | solution.py:28
  63.0 1.1 broadcast_in_dim.33
  64.1 2.0 copy-done.1
  66.1 10.0 %fusion.1 = f32[2048,512]{1,0:T(8,128)} fusion(bf16[2048,512]{1,0:T(8,128)(2,1)S(1)} %copy-done.10, pred[256,8,16,128]{3,2,1,0:T(8,128)(4,1)S(1)} %bitcast.40, bf16[256,8,16,128]{3,2,1,0:T(8,128)(2,1)} %bitcast.43), kind=kOutput, calls=%fused_computation.2 | convolution fusion | flops 4299161600 | bytes 18874368 | tf_op jit(solution)/shard_map/dot_general | solution.py:26
  76.2 39.2 %all-gather.5.cloned.1.call-done = bf16[2048,512]{1,0:T(8,128)(2,1)} async-done(((bf16[128,512]{1,0:T(8,128)(2,1)}), bf16[2048,512]{1,0:T(8,128)(2,1)}) %all-gather.5.cloned.1.call-update) | async-done | bytes 2097168 | tf_op jit(solution)/shard_map/all_gather | solution.py:30
  115.4 11.7 %fusion = f32[2048,512]{1,0:T(8,128)} fusion(bf16[2048,512]{1,0:T(8,128)(2,1)} %all-gather.5.cloned.1.call-done, pred[256,8,16,128]{3,2,1,0:T(8,128)(4,1)} %bitcast.41, bf16[256,8,16,128]{3,2,1,0:T(8,128)(2,1)} %bitcast.44), kind=kOutput, calls=%fused_computation.1 | convolution fusion | flops 4299161600 | bytes 18874368 | tf_op jit(solution)/shard_map/dot_general | solution.py:26
  127.1 0.2 all-reduce.3.cloned.1.call-start
  127.3 53.2 %reduce-scatter.3.cloned.1.call-done = f32[128,512]{1,0:T(8,128)} async-done(((f32[2048,512]{1,0:T(8,128)}), f32[128,512]{1,0:T(8,128)}) %reduce-scatter.3.cloned.1.call-update) | async-done | bytes 262160 | tf_op jit(solution)/shard_map/reduce_scatter | solution.py:29
  180.6 1.0 negate_convert_fusion
  181.6 1.3 fusion.13
  182.9 1.3 convolution_bitcast_fusion.1
  184.2 59.9 %reduce-scatter.5.cloned.1.call-done = f32[128,512]{1,0:T(8,128)} async-done(((f32[2048,512]{1,0:T(8,128)}), f32[128,512]{1,0:T(8,128)}) %reduce-scatter.5.cloned.1.call-update) | async-done | bytes 262160 | tf_op jit(solution)/shard_map/reduce_scatter | solution.py:31
  244.1 1.2 fusion.9
  245.3 1.3 fusion.14
  247.2 266.5 %all-reduce.3.cloned.1.call-done = (f32[512,512]{0,1:T(8,128)}, f32[512,512]{1,0:T(8,128)}, f32[512,512]{0,1:T(8,128)}) async-done(((f32[512,512]{0,1:T(8,128)}, f32[512,512]{1,0:T(8,128)}, f32[512,512]{0,1:T(8,128)}), (f32[512,512]{0,1:T(8,128)}, f32[512,512]{1,0:T(8,128)}, f32[512,512]{0,1:T(8,128)})) %all-reduce.3.cloned.1.call-update) | async-done | bytes 3145744 | tf_op jit(solution)/shard_map/psum | solution.py:39
  513.7 1.5 fusion.10
  515.1 2.6 fusion.5
  517.7 0.5 fusion.6
  518.2 1.0 copy.17
  519.2 1.0 copy.16
  (32 shorter events, 0.7 us)
Async XLA Ops:
  7.2 237.0 %copy-start = (bf16[512,512]{1,0:T(8,128)(2,1)S(1)}, bf16[512,512]{1,0:T(8,128)(2,1)}, u32[]{:S(2)}) copy-start(bf16[512,512]{1,0:T(8,128)(2,1)} %param.12) | copy-start | bytes 1572868
  7.2 55.8 %all-gather.3.cloned.1.call-start = ((), (), s32[]{:S(2)}) async-start(), calls=%async_computation.2 | async-start | bytes 2228224 | tf_op jit(solution)/shard_map/all_gather | solution.py:28
  7.9 107.5 %all-gather.5.cloned.1.call-start = ((), (), s32[]{:S(2)}) async-start(), calls=%async_computation.4 | async-start | bytes 2228224 | tf_op jit(solution)/shard_map/all_gather | solution.py:30
  10.3 170.3 %reduce-scatter.3.cloned.1.call-start = ((), (), s32[]{:S(2)}) async-start(), calls=%async_computation.3 | async-start | bytes 4456448 | tf_op jit(solution)/shard_map/reduce_scatter | solution.py:29
  63.0 3.1 copy-start.10
  64.1 2.0 copy-start.1
  76.1 168.0 %reduce-scatter.5.cloned.1.call-start = ((), (), s32[]{:S(2)}) async-start(), calls=%async_computation.5 | async-start | bytes 4456448 | tf_op jit(solution)/shard_map/reduce_scatter | solution.py:31
  127.1 54.5 %copy-start.2 = (bf16[128,512]{1,0:T(8,128)(2,1)S(1)}, bf16[128,512]{1,0:T(8,128)(2,1)}, u32[]{:S(2)}) copy-start(bf16[128,512]{1,0:T(8,128)(2,1)} %broadcast_select_fusion) | copy-start | bytes 393220
  127.1 55.8 %copy-start.6 = (bf16[128,512]{1,0:T(8,128)(2,1)S(1)}, bf16[128,512]{1,0:T(8,128)(2,1)}, u32[]{:S(2)}) copy-start(bf16[128,512]{1,0:T(8,128)(2,1)} %param.10) | copy-start | bytes 393220
  127.1 119.6 %copy-start.7 = (bf16[512,512]{1,0:T(8,128)(2,1)S(1)}, bf16[512,512]{1,0:T(8,128)(2,1)}, u32[]{:S(2)}) copy-start(bf16[512,512]{1,0:T(8,128)(2,1)} %param.14) | copy-start | bytes 1572868
  127.1 386.5 %all-reduce.3.cloned.1.call-start = ((), (), s32[]{:S(2)}) async-start(), calls=%async_computation.6 | async-start | bytes 6291456 | tf_op jit(solution)/shard_map/psum | solution.py:39
  181.5 65.4 %copy-start.4 = (bf16[128,512]{1,0:T(8,128)(2,1)}, bf16[128,512]{1,0:T(8,128)(2,1)S(1)}, u32[]{:S(2)}) copy-start(bf16[128,512]{1,0:T(8,128)(2,1)S(1)} %negate_convert_fusion) | copy-start | bytes 393220
  182.9 64.0 %copy-start.8 = (bf16[512,512]{1,0:T(8,128)(2,1)S(1)}, bf16[512,512]{1,0:T(8,128)(2,1)}, u32[]{:S(2)}) copy-start(bf16[512,512]{1,0:T(8,128)(2,1)} %param.15) | copy-start | bytes 1572868
  245.3 269.8 %copy-start.9 = (bf16[128,512]{1,0:T(8,128)(2,1)}, bf16[128,512]{1,0:T(8,128)(2,1)S(1)}, u32[]{:S(2)}) copy-start(bf16[128,512]{1,0:T(8,128)(2,1)S(1)} %fusion.9) | copy-start | bytes 393220
  513.7 4.1 copy-start.5
  517.7 2.5 copy-start.3
Sparse Core Ops, SparseCore 0:
  10.4 52.4 all-gather.2
  66.0 49.3 all-gather.4
  117.9 62.5 reduce-scatter.2
  183.0 61.1 reduce-scatter.4
  249.7 263.8 all-reduce.2
where the time goes:
time: 527 us
  waiting for transfers between devices  472 us (90%)
  matrix products  29.8 us (6%)
  between operations  13.9 us (3%)
  local copies, waits for them, and re-layouts  5.61 us (1%)
  other arithmetic  5.46 us (1%)
    psum x1, waiting for transfers between devices, on_device(): own_sum, cross_sum = lax.psum((own_term, cross_local), ('prow', 'pcol'))  266 us
    reduce_scatter x1, waiting for transfers between devices, on_device(): lax.psum_scatter(partial_two, 'pcol', scatter_dimension=0, tiled=True)  59.9 us
    reduce_scatter x1, waiting for transfers between devices, on_device(): lax.psum_scatter(partial_one, 'pcol', scatter_dimension=0, tiled=True)  53.2 us
    all_gather x1, waiting for transfers between devices, on_device(): lax.all_gather(panel_one, 'prow', axis=0, tiled=True)  51.9 us
    all_gather x1, waiting for transfers between devices, on_device(): lax.all_gather(masked_two, 'prow', axis=0, tiled=True)  39.2 us
    dot_general x2, matrix products, accumulate(): return jnp.dot(masked, pieces, preferred_element_type=jnp.float32)  21.7 us
  transfers between devices with their start and end apart: 5, of which 5 were waited for; matrix products, arithmetic and copies ran while one was open for 6% of the time, Pallas kernels for 0%

commit v1 on v0

--- a/solution.py
+++ b/solution.py
@@ -36,7 +36,7 @@
     inverse_two = jnp.where(row_flags, lower_two, jnp.zeros_like(lower_two)).astype(jnp.bfloat16)
     tail_local = jnp.dot(masked_two.T, inverse_two, preferred_element_type=jnp.float32)
     top_weights = panel_top.astype(jnp.float32)
-    own_sum, cross_sum = lax.psum((own_term, cross_local), ("prow", "pcol"))
+    own_sum, cross_sum = lax.psum(lax.psum((own_term, cross_local), "prow"), "pcol")
     corner_full = diag_one.astype(jnp.float32) - own_sum
     top_value = jnp.dot(corner_full, top_weights, precision=lax.Precision.HIGHEST) + cross_sum
     inverse_top = (-top_value).astype(jnp.bfloat16)

time: 527 us -> 747 us (1.42)
  waiting for transfers between devices: 472 us -> 689 us
    psum x1 -> x3, waiting for transfers between devices: 266 us -> 462 us  [the longest x1 257 us: on_device(): tail_sum = lax.psum(tail_local, ('prow', 'pcol'))]
    reduce_scatter x1, waiting for transfers between devices: 53.2 us -> 60.9 us  [on_device(): lax.psum_scatter(partial_one, 'pcol', scatter_dimension=0, tiled=True)]
  transfers between devices with their start and end apart: 5 -> 7, of which waited for: 5 -> 7; matrix products, arithmetic and copies ran while one was open for 6% -> 3% of each run, Pallas kernels for 0% -> 0%
where the time goes in v1:
time: 747 us; the launch traced here: 746 us
  waiting for transfers between devices  689 us (92%)
  matrix products  32.1 us (4%)
  between operations  14.3 us (2%)
    psum x1, waiting for transfers between devices, on_device(): tail_sum = lax.psum(tail_local, ('prow', 'pcol'))  257 us
    psum x1, waiting for transfers between devices, on_device(): lax.psum(lax.psum((own_term, cross_local), 'prow'), 'pcol')  114 us
    psum x1, waiting for transfers between devices, on_device(): lax.psum((own_term, cross_local), 'prow')  91.3 us
    reduce_scatter x1, waiting for transfers between devices, on_device(): lax.psum_scatter(partial_two, 'pcol', scatter_dimension=0, tiled=True)  64.5 us
    reduce_scatter x1, waiting for transfers between devices, on_device(): lax.psum_scatter(partial_one, 'pcol', scatter_dimension=0, tiled=True)  60.9 us
    all_gather x1, waiting for transfers between devices, on_device(): lax.all_gather(panel_one, 'prow', axis=0, tiled=True)  54.3 us
    all_gather x1, waiting for transfers between devices, on_device(): lax.all_gather(masked_two, 'prow', axis=0, tiled=True)  46.6 us
    dot_general x2, matrix products, accumulate(): return jnp.dot(masked, pieces, preferred_element_type=jnp.float32)  21.7 us
  transfers between devices with their start and end apart: 7, of which 7 were waited for; matrix products, arithmetic and copies ran while one was open for 3% of the time, Pallas kernels for 0%

profile of v1, /device:TPU:8, one launch (start us, length us, event | category | flops | bytes accessed | tf_op | source)
XLA Modules:
  0.0 746.3 jit_solution(9237947838078783242)
XLA Ops:
  7.2 0.7 all-gather.3.cloned.1.call-update
  8.0 0.7 broadcast_compare_fusion
  8.7 54.3 %all-gather.3.cloned.1.call-done = bf16[2048,512]{1,0:T(8,128)(2,1)} async-done(((bf16[128,512]{1,0:T(8,128)(2,1)}), bf16[2048,512]{1,0:T(8,128)(2,1)}) %all-gather.3.cloned.1.call-update) | async-done | bytes 2097168 | tf_op jit(solution)/shard_map/all_gather | solution.py:28
  63.0 1.1 broadcast_in_dim.33
  64.1 1.9 copy-done.1
  66.1 10.0 %fusion.1 = f32[2048,512]{1,0:T(8,128)} fusion(bf16[2048,512]{1,0:T(8,128)(2,1)S(1)} %copy-done.10, pred[256,8,16,128]{3,2,1,0:T(8,128)(4,1)S(1)} %bitcast.40, bf16[256,8,16,128]{3,2,1,0:T(8,128)(2,1)} %bitcast.43), kind=kOutput, calls=%fused_computation.2 | convolution fusion | flops 4299161600 | bytes 18874368 | tf_op jit(solution)/shard_map/dot_general | solution.py:26
  77.0 0.7 broadcast_select_fusion
  77.8 60.9 %reduce-scatter.3.cloned.1.call-done = f32[128,512]{1,0:T(8,128)} async-done(((f32[2048,512]{1,0:T(8,128)}), f32[128,512]{1,0:T(8,128)}) %reduce-scatter.3.cloned.1.call-update) | async-done | bytes 262160 | tf_op jit(solution)/shard_map/reduce_scatter | solution.py:29
  138.7 1.0 negate_convert_fusion
  139.7 1.4 convolution_bitcast_fusion.1
  141.0 2.2 fusion.13
  143.3 46.6 %all-gather.5.cloned.1.call-done = bf16[2048,512]{1,0:T(8,128)(2,1)} async-done(((bf16[128,512]{1,0:T(8,128)(2,1)}), bf16[2048,512]{1,0:T(8,128)(2,1)}) %all-gather.5.cloned.1.call-update) | async-done | bytes 2097168 | tf_op jit(solution)/shard_map/all_gather | solution.py:30
  189.9 11.8 %fusion = f32[2048,512]{1,0:T(8,128)} fusion(bf16[2048,512]{1,0:T(8,128)(2,1)} %all-gather.5.cloned.1.call-done, pred[256,8,16,128]{3,2,1,0:T(8,128)(4,1)} %bitcast.41, bf16[256,8,16,128]{3,2,1,0:T(8,128)(2,1)} %bitcast.44), kind=kOutput, calls=%fused_computation.1 | convolution fusion | flops 4299161600 | bytes 18874368 | tf_op jit(solution)/shard_map/dot_general | solution.py:26
  201.8 91.3 %all-reduce.10.cloned.1.call-done = (f32[512,512]{0,1:T(8,128)}, f32[512,512]{1,0:T(8,128)}) async-done(((f32[512,512]{0,1:T(8,128)}, f32[512,512]{1,0:T(8,128)}), (f32[512,512]{0,1:T(8,128)}, f32[512,512]{1,0:T(8,128)})) %all-reduce.10.cloned.1.call-update) | async-done | bytes 2097168 | tf_op jit(solution)/shard_map/psum | solution.py:39
  293.8 64.5 %reduce-scatter.5.cloned.1.call-done = f32[128,512]{1,0:T(8,128)} async-done(((f32[2048,512]{1,0:T(8,128)}), f32[128,512]{1,0:T(8,128)}) %reduce-scatter.5.cloned.1.call-update) | async-done | bytes 262160 | tf_op jit(solution)/shard_map/reduce_scatter | solution.py:31
  358.3 1.2 fusion.9
  359.5 1.3 fusion.14
  360.9 113.6 %all-reduce.8.cloned.1.call-done = (f32[512,512]{0,1:T(8,128)}, f32[512,512]{1,0:T(8,128)}) async-done(((f32[512,512]{0,1:T(8,128)}, f32[512,512]{1,0:T(8,128)}), (f32[512,512]{0,1:T(8,128)}, f32[512,512]{1,0:T(8,128)})) %all-reduce.8.cloned.1.call-update) | async-done | bytes 2097168 | tf_op jit(solution)/shard_map/psum | solution.py:39
  474.5 1.4 fusion.10
  475.9 1.0 copy.16
  476.9 2.6 fusion.5
  479.5 257.2 %all-reduce.6.cloned.1.call-done = f32[512,512]{0,1:T(8,128)} async-done(((f32[512,512]{0,1:T(8,128)}), f32[512,512]{0,1:T(8,128)}) %all-reduce.6.cloned.1.call-update) | async-done | bytes 1048592 | tf_op jit(solution)/shard_map/psum | solution.py:43
  736.7 1.7 fusion.6
  738.4 1.0 copy.17
  (40 shorter events, 1.9 us)
Async XLA Ops:
  7.2 351.1 %copy-start = (bf16[512,512]{1,0:T(8,128)(2,1)S(1)}, bf16[512,512]{1,0:T(8,128)(2,1)}, u32[]{:S(2)}) copy-start(bf16[512,512]{1,0:T(8,128)(2,1)} %param.12) | copy-start | bytes 1572868
  7.2 55.8 %all-gather.3.cloned.1.call-start = ((), (), s32[]{:S(2)}) async-start(), calls=%async_computation.2 | async-start | bytes 2228224 | tf_op jit(solution)/shard_map/all_gather | solution.py:28
  7.9 130.8 %reduce-scatter.3.cloned.1.call-start = ((), (), s32[]{:S(2)}) async-start(), calls=%async_computation.3 | async-start | bytes 4456448 | tf_op jit(solution)/shard_map/reduce_scatter | solution.py:29
  63.0 3.1 copy-start.10
  64.1 1.9 copy-start.1
  76.1 0.7 copy-start.11
  76.1 0.9 copy-start.9
  76.1 63.6 %copy-start.5 = (bf16[128,512]{1,0:T(8,128)(2,1)S(1)}, bf16[128,512]{1,0:T(8,128)(2,1)}, u32[]{:S(2)}) copy-start(bf16[128,512]{1,0:T(8,128)(2,1)} %param.10) | copy-start | bytes 393220
  76.1 113.9 %all-gather.5.cloned.1.call-start = ((), (), s32[]{:S(2)}) async-start(), calls=%async_computation.4 | async-start | bytes 2228224 | tf_op jit(solution)/shard_map/all_gather | solution.py:30
  77.7 215.4 %all-reduce.10.cloned.1.call-start = ((), (), s32[]{:S(2)}) async-start(), calls=%async_computation.8 | async-start | bytes 4194304 | tf_op jit(solution)/shard_map/psum | solution.py:39
  139.7 218.6 %copy-start.4 = (bf16[128,512]{1,0:T(8,128)(2,1)}, bf16[128,512]{1,0:T(8,128)(2,1)S(1)}, u32[]{:S(2)}) copy-start(bf16[128,512]{1,0:T(8,128)(2,1)S(1)} %negate_convert_fusion) | copy-start | bytes 393220
  143.3 215.1 %reduce-scatter.5.cloned.1.call-start = ((), (), s32[]{:S(2)}) async-start(), calls=%async_computation.5 | async-start | bytes 4456448 | tf_op jit(solution)/shard_map/reduce_scatter | solution.py:31
  201.7 91.7 %copy-start.6 = (bf16[512,512]{1,0:T(8,128)(2,1)S(1)}, bf16[512,512]{1,0:T(8,128)(2,1)}, u32[]{:S(2)}) copy-start(bf16[512,512]{1,0:T(8,128)(2,1)} %param.14) | copy-start | bytes 1572868
  201.7 91.9 %copy-start.7 = (bf16[512,512]{1,0:T(8,128)(2,1)S(1)}, bf16[512,512]{1,0:T(8,128)(2,1)}, u32[]{:S(2)}) copy-start(bf16[512,512]{1,0:T(8,128)(2,1)} %param.15) | copy-start | bytes 1572868
  201.7 157.8 %copy-start.2 = (bf16[128,512]{1,0:T(8,128)(2,1)S(1)}, bf16[128,512]{1,0:T(8,128)(2,1)}, u32[]{:S(2)}) copy-start(bf16[128,512]{1,0:T(8,128)(2,1)} %broadcast_select_fusion) | copy-start | bytes 393220
  201.7 272.8 %all-reduce.8.cloned.1.call-start = ((), (), s32[]{:S(2)}) async-start(), calls=%async_computation.7 | async-start | bytes 4194304 | tf_op jit(solution)/shard_map/psum | solution.py:39
  293.1 443.6 %all-reduce.6.cloned.1.call-start = ((), (), s32[]{:S(2)}) async-start(), calls=%async_computation.6 | async-start | bytes 2097152 | tf_op jit(solution)/shard_map/psum | solution.py:43
  359.5 120.0 %copy-start.8 = (bf16[128,512]{1,0:T(8,128)(2,1)}, bf16[128,512]{1,0:T(8,128)(2,1)S(1)}, u32[]{:S(2)}) copy-start(bf16[128,512]{1,0:T(8,128)(2,1)S(1)} %fusion.9) | copy-start | bytes 393220
  479.5 259.9 %copy-start.3 = (bf16[512,512]{1,0:T(8,128)(2,1)}, bf16[512,512]{1,0:T(8,128)(2,1)S(1)}, u32[]{:S(2)}) copy-start(bf16[512,512]{1,0:T(8,128)(2,1)S(1)} %fusion.5) | copy-start | bytes 1572868
Sparse Core Ops, SparseCore 0:
  10.4 52.4 all-gather.2
  76.2 62.4 reduce-scatter.2
  141.7 48.1 all-gather.4
  193.1 99.9 all-reduce.9
  295.7 62.5 reduce-scatter.4
  360.7 113.7 all-reduce.7
  480.8 255.8 all-reduce.5
